TPU v7x, 32 devices: a whole 2x2x4 slice. The times are simulated.
32 devices in a mesh: groups: 2 (over y), mpo: 4 (over z), sec: 2 (over x), rep: 2 (over core).
Axes of the slice: x: 2, y: 2, z: 4, core: 2. Of those that a mesh axis runs over, the one named last changes fastest.
Arguments:
- start_vector: float32 [4, 1024, 256], P(('groups', 'sec'), 'rep'), parts along dimension 0, may hold values from -6 to 6
- block_rows: int32 [4], P(('groups', 'sec')), parts along dimension 0, may hold values from 1 to 1024, 1536 in all
- left_blocks: bfloat16 [8, 4, 1024, 1024], P('mpo', ('groups', 'sec'), 'rep'), parts along dimension 1, as said below
- right_blocks: bfloat16 [8, 4, 256, 256], P('mpo', ('groups', 'sec')), parts along dimension 1, as said below
Outputs:
- wavefunction: float32 [4, 1024, 256], P(('groups', 'sec'), 'rep'), parts along dimension 0
- energy: float32 [2], P('groups'), parts along dimension 0
- environment: float32 [8, 4, 256, 256], P('mpo', ('groups', 'sec'), 'rep'), parts along dimension 1
There are 2 independent parts, one for each index of `groups`. A program takes and returns all parts, laid end to end along the dimension named above; each array names one. Nothing has to cross between parts.
Inputs may be any that keep to these rules, and one draw needn't show every extreme that they name: Each block left_blocks[w, s] is symmetric. Each block right_blocks[w, s] is symmetric.
All inputs are finite; a program needn't handle non-finite values. No bound on the sum of `block_rows` on one device may be relied on, other than what follows from the above.
Results may differ from a plain program's by a relative error of at most 0.017.
Values may be sent and summed in bfloat16 or wider, within the bound.
A program may use at most 64 MiB of HBM per device.

v0:
```python
import math

import jax
import jax.numpy as jnp
from jax import lax
from jax.sharding import PartitionSpec as P

ITERS = 4


EPSILON = 1e-06


def local(start_vector, block_rows, left_blocks, right_blocks):
    sector_count, device_rows, columns = start_vector.shape
    term_count = left_blocks.shape[0]
    block_size = left_blocks.shape[3]
    rep_at = lax.axis_index("rep")
    offset_at = rep_at * device_rows
    row_ids = offset_at + jnp.arange(device_rows, dtype=jnp.int32)
    live_rows = (row_ids[None, :] < block_rows[:, None]).astype(jnp.float32)[:, :, None]

    def summed_over(values):
        stacked = jnp.stack(values)
        return lax.psum(stacked, ("sec", "rep"))

    def apply_left(narrow):
        return jnp.einsum(
            "wsij,sjc->wsic",
            left_blocks,
            lax.all_gather(narrow, "rep", axis=1, tiled=True),
            preferred_element_type=jnp.float32,
        )

    def matvec(vector):
        narrow = vector.astype(jnp.bfloat16)
        partial_left = apply_left(narrow).astype(jnp.bfloat16)
        partial_term = jnp.einsum(
            "wsic,wscd->sid", partial_left, right_blocks, preferred_element_type=jnp.float32
        )
        summed = lax.psum(partial_term.astype(jnp.bfloat16), "mpo").astype(jnp.float32)
        return live_rows * summed

    masked = live_rows * start_vector
    start_norm = summed_over([jnp.sum(masked * masked)])[0]
    vector = masked / jnp.sqrt(start_norm + EPSILON)
    applied = matvec(vector)
    rayleigh = summed_over([jnp.sum(vector * applied)])[0]
    for iteration in range(ITERS):
        residual = applied - rayleigh * vector
        local_square = jnp.sum(residual * residual)
        square_sum = summed_over([local_square])[0]
        image = matvec(residual)
        product_sum = summed_over([jnp.sum(residual * image)])[0]
        scale = jnp.sqrt(square_sum + EPSILON)
        coupling = square_sum / scale
        curvature = product_sum / (scale * scale)
        half_gap = 0.5 * (rayleigh - curvature)
        lowest = 0.5 * (rayleigh + curvature) - jnp.sqrt(half_gap * half_gap + coupling * coupling)
        retain = lowest - curvature
        length = jnp.sqrt(retain * retain + coupling * coupling)
        vector = (retain * vector + coupling * residual / scale) / length
        applied = (retain * applied + coupling * image / scale) / length
        rayleigh = lowest
    all_sectors = lax.axis_size("sec") * sector_count
    final_local = vector * math.sqrt(all_sectors * block_size * columns)
    narrow = final_local.astype(jnp.bfloat16)
    product = apply_left(narrow).astype(jnp.bfloat16)
    env_scale = math.sqrt(term_count * lax.axis_size("mpo") / block_size)
    partial_env = (
        jnp.einsum("sic,wsid->wscd", narrow, product, preferred_element_type=jnp.float32)
        * env_scale
    )
    environment = lax.psum_scatter(
        partial_env.astype(jnp.bfloat16), "rep", scatter_dimension=2, tiled=True
    ).astype(jnp.float32)
    return (final_local, jnp.reshape(rayleigh, (1,)), environment)


def solution(mesh):
    return jax.shard_map(
        local,
        mesh=mesh,
        in_specs=(
            P(("groups", "sec"), "rep", None),
            P(("groups", "sec")),
            P("mpo", ("groups", "sec"), "rep", None),
            P("mpo", ("groups", "sec"), None, None),
        ),
        out_specs=(
            P(("groups", "sec"), "rep", None),
            P("groups"),
            P("mpo", ("groups", "sec"), "rep", None),
        ),
        check_vma=False,
    )
```

profile of v0, /device:TPU:0, one launch (start us, length us, event | category | flops | bytes accessed | tf_op | source)
XLA Modules:
  0.0 306.2 jit_solution(8246175243013970473)
XLA Ops:
  8.0 1.2 copy.21
  9.3 0.7 multiply_reduce_fusion.9
  10.0 8.9 %psum.105 = f32[1]{0:T(128)} all-reduce(f32[1]{0:T(128)} %bitcast.1), channel_id=1, replica_groups=mesh['groups'=2,'mpo'=4,'sec'=2,'rep'=2] {'sec','rep'}, use_global_device_ids=true, to_apply=%region_1.0 | all-reduce | flops 1 | bytes 8 | tf_op jit(solution)/shard_map/psum | solution.py:25
  19.7 0.1 fusion.111
  19.7 2.2 all_gather.18
  21.9 1.7 fusion.84
  23.6 0.0 all-reduce.12.cloned.1.call-start
  23.7 35.7 %all-reduce.10.cloned.1.call-done = bf16[1,512,256]{1,2,0:T(8,128)(2,1)} async-done(((bf16[1,512,256]{1,2,0:T(8,128)(2,1)}), bf16[1,512,256]{1,2,0:T(8,128)(2,1)}) %all-reduce.10.cloned.1.call-update) | async-done | bytes 262160 | tf_op jit(solution)/shard_map/psum | solution.py:41
  59.4 1.7 multiply_reduce_fusion.8
  61.1 6.3 %psum.107 = f32[]{:T(128)} all-reduce(f32[]{:T(128)} %multiply_reduce_fusion.8), channel_id=1, replica_groups=mesh['groups'=2,'mpo'=4,'sec'=2,'rep'=2] {'sec','rep'}, use_global_device_ids=true, to_apply=%region_4.0 | all-reduce | flops 1 | bytes 8 | tf_op jit(solution)/shard_map/psum | solution.py:25
  67.4 1.7 fusion.108
  69.1 2.2 all_gather.19
  71.3 2.6 fusion.81
  74.0 0.0 all-reduce.14.cloned.1.call-start
  74.0 35.5 %all-reduce.12.cloned.1.call-done = bf16[1,512,256]{1,2,0:T(8,128)(2,1)} async-done(((bf16[1,512,256]{1,2,0:T(8,128)(2,1)}), bf16[1,512,256]{1,2,0:T(8,128)(2,1)}) %all-reduce.12.cloned.1.call-update) | async-done | bytes 262160 | tf_op jit(solution)/shard_map/psum | solution.py:41
  109.5 2.4 multiply_reduce_fusion.6
  111.9 6.3 %all-reduce.3 = (f32[]{:T(128)}, f32[]{:T(128)}) all-reduce(f32[]{:T(128)} %get-tuple-element.12, f32[]{:T(128)} %get-tuple-element.11), channel_id=1, replica_groups=mesh['groups'=2,'mpo'=4,'sec'=2,'rep'=2] {'sec','rep'}, use_global_device_ids=true, to_apply=%region_7.0 | all-reduce | flops 2 | bytes 16 | tf_op jit(solution)/shard_map/psum | solution.py:25
  121.5 1.9 fusion.114
  123.4 2.3 all_gather.20
  125.8 2.8 fusion.78
  128.5 0.0 all-reduce.16.cloned.1.call-start
  128.6 35.4 %all-reduce.14.cloned.1.call-done = bf16[1,512,256]{1,2,0:T(8,128)(2,1)} async-done(((bf16[1,512,256]{1,2,0:T(8,128)(2,1)}), bf16[1,512,256]{1,2,0:T(8,128)(2,1)}) %all-reduce.14.cloned.1.call-update) | async-done | bytes 262160 | tf_op jit(solution)/shard_map/psum | solution.py:41
  164.0 1.8 multiply_reduce_fusion.4
  165.8 6.3 %all-reduce.2 = (f32[]{:T(128)}, f32[]{:T(128)}) all-reduce(f32[]{:T(128)} %get-tuple-element.16, f32[]{:T(128)} %get-tuple-element.15), channel_id=1, replica_groups=mesh['groups'=2,'mpo'=4,'sec'=2,'rep'=2] {'sec','rep'}, use_global_device_ids=true, to_apply=%region_12.0 | all-reduce | flops 2 | bytes 16 | tf_op jit(solution)/shard_map/psum | solution.py:25
  174.2 3.2 %fusion.110 = (bf16[1,512,256]{1,2,0:T(8,128)(2,1)S(1)}, f32[1,512,256]{1,2,0:T(8,128)S(1)}, f32[1,512,256]{1,2,0:T(8,128)}) fusion(f32[]{:T(128)S(6)} %sub.54, f32[]{:T(128)S(6)} %sqrt.49, f32[]{:T(128)S(6)} %sqrt.47, f32[1,512,256]{1,2,0:T(8,128)} %copy-done.3, f32[]{:T(128)S(6)} %div.113, f32[]{:T(128)S(6)} %sqrt.46, f32[]{:T(128)S(6)} %sqrt.44, ...), kind=kLoop, calls=%fused_computation.83 | loop fusion | flops 4325376 | bytes 3147820 | tf_op jit(solution)/shard_map/convert_element_type | solution.py:36
  177.3 2.3 all_gather.21
  179.6 2.8 fusion.75
  182.5 0.0 all-reduce.18.cloned.1.call-start
  182.5 35.5 %all-reduce.16.cloned.1.call-done = bf16[1,512,256]{1,2,0:T(8,128)(2,1)} async-done(((bf16[1,512,256]{1,2,0:T(8,128)(2,1)}), bf16[1,512,256]{1,2,0:T(8,128)(2,1)}) %all-reduce.16.cloned.1.call-update) | async-done | bytes 262160 | tf_op jit(solution)/shard_map/psum | solution.py:41
  218.0 1.7 multiply_reduce_fusion.2
  219.7 6.3 %all-reduce.1 = (f32[]{:T(128)}, f32[]{:T(128)}) all-reduce(f32[]{:T(128)} %get-tuple-element.10, f32[]{:T(128)} %get-tuple-element.9), channel_id=1, replica_groups=mesh['groups'=2,'mpo'=4,'sec'=2,'rep'=2] {'sec','rep'}, use_global_device_ids=true, to_apply=%region_17.0 | all-reduce | flops 2 | bytes 16 | tf_op jit(solution)/shard_map/psum | solution.py:25
  228.1 2.0 fusion.113
  230.1 2.3 all_gather.22
  232.4 2.7 fusion.72
  235.2 0.0 reduce-scatter.4.cloned.1.call-start
  235.2 35.4 %all-reduce.18.cloned.1.call-done = bf16[1,512,256]{1,2,0:T(8,128)(2,1)} async-done(((bf16[1,512,256]{1,2,0:T(8,128)(2,1)}), bf16[1,512,256]{1,2,0:T(8,128)(2,1)}) %all-reduce.18.cloned.1.call-update) | async-done | bytes 262160 | tf_op jit(solution)/shard_map/psum | solution.py:41
  270.6 1.9 multiply_reduce_fusion
  272.5 6.3 %all-reduce = (f32[]{:T(128)}, f32[]{:T(128)}) all-reduce(f32[]{:T(128)} %get-tuple-element.14, f32[]{:T(128)} %get-tuple-element.13), channel_id=1, replica_groups=mesh['groups'=2,'mpo'=4,'sec'=2,'rep'=2] {'sec','rep'}, use_global_device_ids=true, to_apply=%region_22.0 | all-reduce | flops 2 | bytes 16 | tf_op jit(solution)/shard_map/psum | solution.py:25
  280.8 2.1 fusion.112
  282.9 2.2 all_gather.23
  285.1 1.6 fusion.87
  286.7 1.1 copy.52
  287.8 0.7 copy.54
  288.6 1.0 copy.33
  289.6 6.8 %reduce-scatter.4.cloned.1.call-done = bf16[128,512]{1,0:T(8,128)(2,1)} async-done(((bf16[256,512]{1,0:T(8,128)(2,1)}), bf16[128,512]{1,0:T(8,128)(2,1)}) %reduce-scatter.4.cloned.1.call-update) | async-done | bytes 131088
  296.4 0.9 reshape.144
  297.3 0.1 copy.53
  297.5 0.8 copy.34
  (22 shorter events, 0.2 us)
Async XLA Ops:
  7.2 14.8 %copy-start = (bf16[2,1,512,1024]{3,2,1,0:T(8,128)(2,1)S(1)}, bf16[2,1,512,1024]{3,2,1,0:T(8,128)(2,1)}, u32[]{:S(2)}) copy-start(bf16[2,1,512,1024]{3,2,1,0:T(8,128)(2,1)} %param.6) | copy-start | bytes 6291460
  7.2 14.8 %copy-start.5 = (bf16[2,1,256,256]{3,2,1,0:T(8,128)(2,1)S(1)}, bf16[2,1,256,256]{3,2,1,0:T(8,128)(2,1)}, u32[]{:S(2)}) copy-start(bf16[2,1,256,256]{3,2,1,0:T(8,128)(2,1)} %param.7) | copy-start | bytes 786436
  7.2 52.2 %all-reduce.10.cloned.1.call-start = ((), (), s32[]{:S(2)}) async-start(), calls=%async_computation.1 | async-start | bytes 524288 | tf_op jit(solution)/shard_map/psum | solution.py:41
  23.6 85.9 %all-reduce.12.cloned.1.call-start = ((), (), s32[]{:S(2)}) async-start(), calls=%async_computation.2 | async-start | bytes 524288 | tf_op jit(solution)/shard_map/psum | solution.py:41
  71.3 38.2 %copy-start.2 = (bf16[1,512,256]{1,2,0:T(8,128)(2,1)S(1)}, bf16[1,512,256]{1,2,0:T(8,128)(2,1)}, u32[]{:S(2)}) copy-start(bf16[1,512,256]{1,2,0:T(8,128)(2,1)} %all-reduce.10.cloned.1.call-done) | copy-start | bytes 786436
  74.0 90.1 %all-reduce.14.cloned.1.call-start = ((), (), s32[]{:S(2)}) async-start(), calls=%async_computation.3 | async-start | bytes 524288 | tf_op jit(solution)/shard_map/psum | solution.py:41
  123.4 40.6 %copy-start.3 = (f32[1,512,256]{1,2,0:T(8,128)}, f32[1,512,256]{1,2,0:T(8,128)S(1)}, u32[]{:S(2)}) copy-start(f32[1,512,256]{1,2,0:T(8,128)S(1)} %get-tuple-element.33) | copy-start | bytes 1572868
  128.5 89.4 %all-reduce.16.cloned.1.call-start = ((), (), s32[]{:S(2)}) async-start(), calls=%async_computation.4 | async-start | bytes 524288 | tf_op jit(solution)/shard_map/psum | solution.py:41
  179.6 38.4 %copy-start.1 = (f32[1,512,256]{1,2,0:T(8,128)S(1)}, f32[1,512,256]{1,2,0:T(8,128)}, u32[]{:S(2)}) copy-start(f32[1,512,256]{1,2,0:T(8,128)} %get-tuple-element.31) | copy-start | bytes 1572868
  182.5 88.1 %all-reduce.18.cloned.1.call-start = ((), (), s32[]{:S(2)}) async-start(), calls=%async_computation.5 | async-start | bytes 524288 | tf_op jit(solution)/shard_map/psum | solution.py:41
  218.0 14.5 %copy-start.6 = (bf16[2,1,256,256]{3,2,1,0:T(8,128)(2,1)S(1)}, bf16[2,1,256,256]{3,2,1,0:T(8,128)(2,1)}, u32[]{:S(2)}) copy-start(bf16[2,1,256,256]{3,2,1,0:T(8,128)(2,1)} %param.7) | copy-start | bytes 786436
  235.2 61.2 %reduce-scatter.4.cloned.1.call-start = ((), (), s32[]{:S(2)}) async-start(), calls=%async_computation.6 | async-start | bytes 393216
  285.1 3.5 %copy-start.4 = (f32[1,512,256]{1,2,0:T(8,128)S(1)}, f32[1,512,256]{1,2,0:T(8,128)}, u32[]{:S(2)}) copy-start(f32[1,512,256]{1,2,0:T(8,128)} %get-tuple-element.26) | copy-start | bytes 1572868
Sparse Core Ops, SparseCore 0:
  23.7 35.6 all-reduce.9
  74.1 35.3 all-reduce.11
  128.7 35.3 all-reduce.13
  182.6 35.3 all-reduce.15
  235.3 35.2 all-reduce.17
  288.7 7.6 reduce-scatter.3
where the time goes:
time: 307 us; the launch traced here: 306 us
  waiting for transfers between devices  184 us (60%)
  blocking collectives  53.8 us (18%)
  between operations  26.5 us (9%)
  other arithmetic  21.2 us (7%)
  matrix products  14.2 us (5%)
  local copies, waits for them, and re-layouts  6.03 us (2%)
    psum x5, waiting for transfers between devices, matvec(): lax.psum(partial_term.astype(jnp.bfloat16), 'mpo').astype(jnp.float32)  177 us
    psum x6, blocking collectives, summed_over(): return lax.psum(stacked, ('sec', 'rep'))  40.4 us
    all_gather x6, blocking collectives, apply_left(): lax.all_gather(narrow, 'rep', axis=1, tiled=True)  13.4 us
    dot_general x5, matrix products, matvec(): jnp.einsum('wsic,wscd->sid', partial_left, right_blocks, preferred_elemen...  12.6 us
    convert_element_type x5, other arithmetic, matvec(): narrow = vector.astype(jnp.bfloat16)  8.89 us
    reduce_sum x4, other arithmetic, local(): local_square = jnp.sum(residual * residual)  7.75 us
    unnamed x7, waiting for transfers between devices  6.92 us
  transfers between devices with their start and end apart: 6, of which 6 were waited for; matrix products, arithmetic and copies ran while one was open for 0% of the time, Pallas kernels for 0%

commit v1 on v0

v1 whole, which is shorter than its diff:
```python
import functools
import math

import jax
import jax.numpy as jnp
from jax import lax
from jax.experimental import pallas as pl
from jax.experimental.pallas import tpu as pltpu
from jax.sharding import PartitionSpec as P

ITERS = 4
EPSILON = 1e-06
STEPS = ITERS + 1
CHUNKS = 8
BLOCKS = 4
LAG = 2

F32 = jnp.float32
BF16 = jnp.bfloat16
MESH = pl.DeviceIdType.MESH


def body(
    n_mpo, n_sec, block_rows, start_hbm, left_hbm, right_hbm,
    wave_ref, energy_ref, env_ref,
    start_v, left, right, u, x, prod, term, inward, sums, total, got_in, got_out,
    acc, gram, last, env_own, env_send, env_recv,
    load_sem, x_send, x_recv, in_send, in_recv, out_send, out_recv,
    gram_send, gram_recv, last_send, last_recv, env_send_sem, env_recv_sem,
):
    terms, rows, size = left.shape
    cols = right.shape[1]
    chunk = rows // CHUNKS
    block = rows // BLOCKS
    per_block = CHUNKS // BLOCKS
    n_rep = 2
    n_peer = n_sec * n_rep
    n_all = n_mpo * n_peer
    half = n_mpo // 2

    z = lax.axis_index("mpo")
    sec = lax.axis_index("sec")
    rep = lax.axis_index("rep")
    peer = sec * n_rep + rep
    every = z * n_peer + peer
    other = 1 - rep
    lower = z < half
    depth = jnp.where(lower, z, n_mpo - 1 - z)
    z_in = jnp.where(lower, z + 1, z - 1)
    z_out = jnp.where(lower, z - 1, z + 1)
    middle = depth == half - 1
    outer = depth == 0
    own_at = pl.multiple_of(rep * rows, rows)
    other_at = pl.multiple_of(other * rows, rows)

    def device_at(index):
        return {
            "mpo": index // n_peer,
            "sec": lax.rem(index, n_peer) // n_rep,
            "rep": lax.rem(index, n_rep),
        }

    start_load = pltpu.make_async_copy(start_hbm.at[0], start_v, load_sem.at[0])
    left_load = pltpu.make_async_copy(left_hbm.at[:, 0], left, load_sem.at[1])
    right_load = pltpu.make_async_copy(right_hbm.at[:, 0], right, load_sem.at[2])
    start_load.start()
    left_load.start()
    right_load.start()

    barrier = pltpu.get_barrier_semaphore()

    def greet(d, carry):
        target = lax.rem(every + d, n_all)
        pl.semaphore_signal(barrier, inc=1, device_id=device_at(target), device_id_type=MESH)
        return carry

    lax.fori_loop(1, n_all, greet, 0)

    live_count = block_rows[0] - rep * rows
    row_at = lax.broadcasted_iota(jnp.int32, (chunk, cols), 0)

    def live_of(c):
        return row_at + c * chunk < live_count

    def x_copy(k, at, count):
        return pltpu.make_async_remote_copy(
            src_ref=x.at[k, pl.ds(at, count)],
            dst_ref=x.at[k, pl.ds(at, count)],
            send_sem=x_send.at[k],
            recv_sem=x_recv.at[k],
            device_id={"rep": other},
            device_id_type=MESH,
        )

    def in_copy(k, c, to_middle):
        if to_middle:
            return pltpu.make_async_remote_copy(
                src_ref=sums.at[k, c], dst_ref=got_out.at[k, c],
                send_sem=in_send.at[k], recv_sem=out_recv.at[k, c],
                device_id={"mpo": z_in}, device_id_type=MESH,
            )
        return pltpu.make_async_remote_copy(
            src_ref=sums.at[k, c], dst_ref=got_in.at[k, c],
            send_sem=in_send.at[k], recv_sem=in_recv.at[k, c],
            device_id={"mpo": z_in}, device_id_type=MESH,
        )

    def out_copy(k, c):
        return pltpu.make_async_remote_copy(
            src_ref=total.at[k, c], dst_ref=got_out.at[k, c],
            send_sem=out_send.at[k], recv_sem=out_recv.at[k, c],
            device_id={"mpo": z_out}, device_id_type=MESH,
        )

    def gram_copy(k, d, sending):
        target = lax.rem(peer + d, n_peer)
        slot = peer if sending else lax.rem(peer - d + n_peer, n_peer)
        return pltpu.make_async_remote_copy(
            src_ref=gram.at[k, slot], dst_ref=gram.at[k, slot],
            send_sem=gram_send.at[k], recv_sem=gram_recv.at[k, d],
            device_id={"sec": target // n_rep, "rep": lax.rem(target, n_rep)},
            device_id_type=MESH,
        )

    def last_copy(d, sending):
        target = lax.rem(every + d, n_all)
        slot = every if sending else lax.rem(every - d + n_all, n_all)
        return pltpu.make_async_remote_copy(
            src_ref=last.at[slot], dst_ref=last.at[slot],
            send_sem=last_send, recv_sem=last_recv.at[d],
            device_id=device_at(target), device_id_type=MESH,
        )

    def send_inward(k, c):
        if n_mpo == 2:
            in_copy(k, c, True).start()
            return

        @pl.when(middle)
        def _():
            in_copy(k, c, True).start()

        @pl.when(jnp.logical_not(middle))
        def _():
            in_copy(k, c, False).start()

    def fold(values):
        return jnp.sum(values.reshape(chunk // 8, 8, cols), axis=0)

    def put_basis(k, c, new):
        at = pl.multiple_of(c * chunk, chunk)
        u[k, pl.ds(at, chunk)] = new
        x_at = pl.multiple_of(own_at + c * chunk, chunk)
        x[k, pl.ds(x_at, chunk)] = new.astype(BF16)
        x_copy(k, x_at, chunk).start()
        for j in range(k):
            acc[j] += fold(new * u[j, pl.ds(at, chunk)])
        acc[k] += fold(new * new)

    def whole(values):
        one = jnp.sum(jnp.sum(values, axis=0, keepdims=True), axis=1, keepdims=True)
        return jnp.broadcast_to(one, (1, cols))

    def share_gram(k):
        parts = [whole(acc[j]) for j in range(k + 1)]
        parts += [jnp.zeros((8 - k - 1, cols), F32)]
        gram[k, peer] = jnp.concatenate(parts, axis=0)
        for d in range(1, n_peer):
            gram_copy(k, d, True).start()

    def take_gram(k):
        for d in range(1, n_peer):
            gram_copy(k, d, False).wait_recv()
        summed = gram[k, 0]
        for slot in range(1, n_peer):
            summed = summed + gram[k, slot]
        return [summed[j : j + 1] for j in range(k + 1)]

    def multiply(k):
        def one(b, carry):
            at = pl.multiple_of(b * block, block)
            for w in range(terms):
                left_term = jnp.dot(
                    left[w, pl.ds(at, block)], x[k], preferred_element_type=F32
                )
                prod[k, pl.ds(at, block), w * cols : (w + 1) * cols] = left_term.astype(BF16)
            group = jnp.dot(
                prod[k, pl.ds(at, block)],
                right[...].reshape(terms * cols, cols),
                preferred_element_type=F32,
            )
            if k < ITERS:
                for i in range(per_block):
                    piece = group[i * chunk : (i + 1) * chunk]
                    c = b * per_block + i

                    @pl.when(outer)
                    def _():
                        sums[k, c] = piece.astype(BF16)
                        send_inward(k, c)

                    @pl.when(jnp.logical_not(outer))
                    def _():
                        term[c] = piece
            else:
                held = group * u[k, pl.ds(at, block)]
                acc[0] += jnp.sum(held.reshape(block // 8, 8, cols), axis=0)
            return carry

        lax.fori_loop(0, BLOCKS, one, 0)

    ups, mids, downs, grams = [], [], [], {}

    def g(i, j):
        return grams[(min(i, j), max(i, j))]

    def coefficients(k):
        here = g(k, k) + EPSILON
        inverse = lax.rsqrt(here)
        if k == 0:
            mid = jnp.zeros_like(here)
            down = jnp.zeros_like(here)
        else:
            before = g(k - 1, k - 1) + EPSILON
            lean = ups[k - 1] * g(k - 1, k)
            if k >= 2:
                lean = lean + downs[k - 1] * g(k - 2, k - 1)
            mid = mids[k - 1] + lean / before
            down = ups[k - 1] * g(k, k) / before
        ups.append(here * inverse)
        mids.append(mid)
        downs.append(down)
        return inverse

    def combine(k, inverse):
        mid, down = mids[k], downs[k]

        def finish(c):
            @pl.when(middle)
            def _():
                out_copy(k, c).wait_recv()
                sides = sums[k, c].astype(F32) + got_out[k, c].astype(F32)
                total[k, c] = sides.astype(BF16)

            @pl.when(jnp.logical_not(middle))
            def _():
                out_copy(k, c).wait_recv()
                total[k, c] = got_out[k, c]

            @pl.when(jnp.logical_not(outer))
            def _():
                out_copy(k, c).start()

            at = pl.multiple_of(c * chunk, chunk)
            applied = jnp.where(live_of(c), total[k, c].astype(F32), 0.0)
            new = applied - mid * u[k, pl.ds(at, chunk)]
            if k >= 1:
                new = new - down * u[k - 1, pl.ds(at, chunk)]
            put_basis(k + 1, c, new * inverse)

        def one(c, carry):
            @pl.when(jnp.logical_and(jnp.logical_not(outer), c < CHUNKS))
            def _():
                in_copy(k, c, False).wait_recv()
                sums[k, c] = (term[c] + got_in[k, c].astype(F32)).astype(BF16)
                send_inward(k, c)

            @pl.when(c >= LAG)
            def _():
                finish(c - LAG)

            return carry

        lax.fori_loop(0, CHUNKS + LAG, one, 0)

    def dot_of(a, b):
        result = None
        for i, left_value in a.items():
            inner = None
            for j, right_value in b.items():
                value = right_value * g(i, j)
                inner = value if inner is None else inner + value
            value = left_value * inner
            result = value if result is None else result + value
        return result

    def applied_to(a):
        result = {}

        def add(i, value):
            result[i] = value if i not in result else result[i] + value

        for k, value in a.items():
            add(k + 1, ups[k] * value)
            if k >= 1:
                add(k, mids[k] * value)
                add(k - 1, downs[k] * value)
        return result

    def mixed(first, a, second, b):
        result = {i: first * value for i, value in a.items()}
        for i, value in b.items():
            scaled = second * value
            result[i] = scaled if i not in result else result[i] + scaled
        return result

    start_load.wait()
    pl.semaphore_wait(barrier, n_all - 1)
    acc[...] = jnp.zeros_like(acc)

    def begin(c, carry):
        at = pl.multiple_of(c * chunk, chunk)
        put_basis(0, c, jnp.where(live_of(c), start_v[pl.ds(at, chunk)], 0.0))
        return carry

    lax.fori_loop(0, CHUNKS, begin, 0)
    share_gram(0)
    left_load.wait()
    right_load.wait()

    state = {}
    for k in range(STEPS):
        x_copy(k, other_at, rows).wait_recv()
        if k == ITERS:
            acc[...] = jnp.zeros_like(acc)
        multiply(k)
        if k == ITERS:
            last[every] = jnp.broadcast_to(whole(acc[0])[:, :128], (8, 128))

            def send_last(d, carry):
                last_copy(d, True).start()
                return carry

            lax.fori_loop(1, n_all, send_last, 0)
        for j, value in enumerate(take_gram(k)):
            grams[(j, k)] = value
        if k < ITERS:
            inverse = coefficients(k)
        if k == 0:
            first = lax.rsqrt(g(0, 0) + EPSILON)
            state["vector"] = {0: first}
            state["applied"] = applied_to(state["vector"])
        if k == 1:
            state["rayleigh"] = dot_of(state["vector"], state["applied"])
        if k >= 1:
            vector, applied, rayleigh = state["vector"], state["applied"], state["rayleigh"]
            if k >= 2:
                residual, square_sum = state["residual"], state["square_sum"]
                scale, coupling = state["scale"], state["coupling"]
                image = applied_to(residual)
                product_sum = dot_of(residual, image)
                curvature = product_sum / (scale * scale)
                half_gap = 0.5 * (rayleigh - curvature)
                lowest = 0.5 * (rayleigh + curvature) - jnp.sqrt(half_gap * half_gap + coupling * coupling)
                retain = lowest - curvature
                length = jnp.sqrt(retain * retain + coupling * coupling)
                one, two = retain / length, coupling / (scale * length)
                vector = mixed(one, vector, two, residual)
                applied = mixed(one, applied, two, image)
                rayleigh = lowest
            residual = mixed(1.0, applied, -rayleigh, vector)
            square_sum = dot_of(residual, residual)
            scale = jnp.sqrt(square_sum + EPSILON)
            state = dict(
                vector=vector, applied=applied, rayleigh=rayleigh, residual=residual,
                square_sum=square_sum, scale=scale, coupling=square_sum / scale,
            )
        if k < ITERS:
            acc[...] = jnp.zeros_like(acc)
            combine(k, inverse)
            share_gram(k + 1)

    vector, rayleigh, residual = state["vector"], state["rayleigh"], state["residual"]
    scale, coupling = state["scale"], state["coupling"]
    top = residual[ITERS]
    lower_part = {i: value for i, value in residual.items() if i < ITERS}
    lower_image = applied_to(lower_part)
    known = dot_of(residual, lower_image) + top * dot_of({ITERS: jnp.ones_like(top)}, lower_image)
    inverse_square = 1.0 / (scale * scale)

    def take_last(d, carry):
        last_copy(d, False).wait_recv()
        return carry

    lax.fori_loop(1, n_all, take_last, 0)
    corner = lax.fori_loop(1, n_all, lambda i, value: value + last[i, 0:1], last[0, 0:1])
    corner = jnp.broadcast_to(corner[:, 0:1], (1, cols))
    curvature = (known + top * top * corner) * inverse_square
    half_gap = 0.5 * (rayleigh - curvature)
    lowest = 0.5 * (rayleigh + curvature) - jnp.sqrt(half_gap * half_gap + coupling * coupling)
    retain = lowest - curvature
    length = jnp.sqrt(retain * retain + coupling * coupling)
    full = math.sqrt(n_sec * size * cols)
    vector = mixed(full * retain / length, vector, full * coupling / (scale * length), residual)
    energy_ref[0] = lowest[0, 0]

    def finish_rows(c, carry):
        at = pl.multiple_of(c * chunk, chunk)
        here = pl.ds(at, chunk)
        wave = vector[0] * u[0, here]
        for k in range(1, STEPS):
            wave = wave + vector[k] * u[k, here]
        wave_ref[0, here] = wave
        x[0, here] = wave.astype(BF16)
        for w in range(terms):
            span = slice(w * cols, (w + 1) * cols)
            image = vector[0] * prod[0, here, span].astype(F32)
            for k in range(1, STEPS):
                image = image + vector[k] * prod[k, here, span].astype(F32)
            prod[0, here, span] = image.astype(BF16)
        return carry

    for k in range(STEPS):
        x_copy(k, own_at, rows).wait_send()
    lax.fori_loop(0, CHUNKS, finish_rows, 0)
    env_scale = math.sqrt(terms * n_mpo / size)
    env = lax.dot_general(
        x[0, 0:rows], prod[0], (((0,), (0,)), ((), ())), preferred_element_type=F32
    ) * env_scale
    env_own[...] = env
    share = cols // n_rep
    env_send[...] = env_own[pl.ds(pl.multiple_of(other * share, share), share)].astype(BF16)
    env_copy = pltpu.make_async_remote_copy(
        src_ref=env_send, dst_ref=env_recv, send_sem=env_send_sem, recv_sem=env_recv_sem,
        device_id={"rep": other}, device_id_type=MESH,
    )
    env_copy.start()

    for k in range(ITERS):
        in_copy_all = pltpu.make_async_remote_copy(
            src_ref=sums.at[k], dst_ref=got_in.at[k], send_sem=in_send.at[k],
            recv_sem=in_recv.at[k, 0], device_id={"mpo": z_in}, device_id_type=MESH,
        )
        in_copy_all.wait_send()

        @pl.when(jnp.logical_not(outer))
        def _():
            pltpu.make_async_remote_copy(
                src_ref=total.at[k], dst_ref=got_out.at[k], send_sem=out_send.at[k],
                recv_sem=out_recv.at[k, 0], device_id={"mpo": z_out}, device_id_type=MESH,
            ).wait_send()

    for k in range(STEPS):
        for d in range(1, n_peer):
            gram_copy(k, d, True).wait_send()

    def done_last(d, carry):
        last_copy(d, True).wait_send()
        return carry

    lax.fori_loop(1, n_all, done_last, 0)

    env_copy.wait()
    kept = env_own[pl.ds(pl.multiple_of(rep * share, share), share)] + env_recv[...].astype(F32)
    for w in range(terms):
        env_ref[w, 0] = kept[:, w * cols : (w + 1) * cols]


def local(n_mpo, n_sec, start_vector, block_rows, left_blocks, right_blocks):
    _, rows, cols = start_vector.shape
    terms, _, _, size = left_blocks.shape
    chunk = rows // CHUNKS
    n_peer = n_sec * 2
    n_all = n_mpo * n_peer
    dma = pltpu.SemaphoreType.DMA
    passing = pltpu.VMEM((ITERS, CHUNKS, chunk, cols), BF16)
    return pl.pallas_call(
        functools.partial(body, n_mpo, n_sec),
        out_shape=(
            jax.ShapeDtypeStruct((1, rows, cols), F32),
            jax.ShapeDtypeStruct((1,), F32),
            jax.ShapeDtypeStruct((terms, 1, cols // 2, cols), F32),
        ),
        in_specs=[
            pl.BlockSpec(memory_space=pltpu.SMEM),
            pl.BlockSpec(memory_space=pl.ANY),
            pl.BlockSpec(memory_space=pl.ANY),
            pl.BlockSpec(memory_space=pl.ANY),
        ],
        out_specs=(
            pl.BlockSpec(memory_space=pltpu.VMEM),
            pl.BlockSpec(memory_space=pltpu.SMEM),
            pl.BlockSpec(memory_space=pltpu.VMEM),
        ),
        scratch_shapes=[
            pltpu.VMEM((rows, cols), F32),
            pltpu.VMEM((terms, rows, size), BF16),
            pltpu.VMEM((terms, cols, cols), BF16),
            pltpu.VMEM((STEPS, rows, cols), F32),
            pltpu.VMEM((STEPS, size, cols), BF16),
            pltpu.VMEM((STEPS, rows, terms * cols), BF16),
            pltpu.VMEM((CHUNKS, chunk, cols), F32),
            pltpu.VMEM((8, 128), F32),
            passing,
            passing,
            passing,
            passing,
            pltpu.VMEM((STEPS, 8, cols), F32),
            pltpu.VMEM((STEPS, n_peer, 8, cols), F32),
            pltpu.VMEM((n_all, 8, 128), F32),
            pltpu.VMEM((cols, terms * cols), F32),
            pltpu.VMEM((cols // 2, terms * cols), BF16),
            pltpu.VMEM((cols // 2, terms * cols), BF16),
            dma((3,)),
            dma((STEPS,)),
            dma((STEPS,)),
            dma((ITERS,)),
            dma((ITERS, CHUNKS)),
            dma((ITERS,)),
            dma((ITERS, CHUNKS)),
            dma((STEPS,)),
            dma((STEPS, n_peer)),
            dma,
            dma((n_all,)),
            dma,
            dma,
        ],
        compiler_params=pltpu.CompilerParams(
            collective_id=0, has_side_effects=True, vmem_limit_bytes=50 * 2**20
        ),
    )(block_rows, start_vector, left_blocks, right_blocks)


def solution(mesh):
    return jax.shard_map(
        functools.partial(local, mesh.shape["mpo"], mesh.shape["sec"]),
        mesh=mesh,
        in_specs=(
            P(("groups", "sec"), "rep", None),
            P(("groups", "sec")),
            P("mpo", ("groups", "sec"), "rep", None),
            P("mpo", ("groups", "sec"), None, None),
        ),
        out_specs=(
            P(("groups", "sec"), "rep", None),
            P("groups"),
            P("mpo", ("groups", "sec"), "rep", None),
        ),
        check_vma=False,
    )
```

time: 307 us -> 90.9 us (0.30)
  waiting for transfers between devices: 184 us -> 0 us
  Pallas kernels: 0 us -> 82.6 us
  blocking collectives: 53.8 us -> 0 us
  between operations: 26.5 us -> 3.04 us
  other arithmetic: 21.2 us -> 0 us
  matrix products: 14.2 us -> 0 us
    psum x5 -> x0, waiting for transfers between devices: 177 us -> none  [matvec(): lax.psum(partial_term.astype(jnp.bfloat16), 'mpo').astype(jnp.float32)]
    pallas_call x0 -> x1, Pallas kernels: none -> 82.6 us  [local(): pl.pallas_call(functools.partial(body, n_mpo, n_sec), out_shape=(jax.Shap...]
    psum x6 -> x0, blocking collectives: 40.4 us -> none  [summed_over(): return lax.psum(stacked, ('sec', 'rep'))]
    dot_general x6 -> x0, matrix products: 14.2 us -> none  [the longest x5 12.6 us: matvec(): jnp.einsum('wsic,wscd->sid', partial_left, right_blocks, preferred_elemen...]
    all_gather x6 -> x0, blocking collectives: 13.4 us -> none  [apply_left(): lax.all_gather(narrow, 'rep', axis=1, tiled=True)]
    convert_element_type x7 -> x0, other arithmetic: 11 us -> none  [the longest x5 8.89 us: matvec(): narrow = vector.astype(jnp.bfloat16)]
    reduce_sum x6 -> x0, other arithmetic: 10.2 us -> none  [the longest x4 7.75 us: local(): local_square = jnp.sum(residual * residual)]
    unnamed x7 -> x0, waiting for transfers between devices: 6.92 us -> none
  transfers between devices with their start and end apart: 6 -> 0, of which waited for: 6 -> 0; matrix products, arithmetic and copies ran while one was open for 0% -> 0% of each run, Pallas kernels for 0% -> 0%
where the time goes in v1:
time: 90.9 us; the launch traced here: 90.7 us
  Pallas kernels  82.6 us (91%)
  local copies, waits for them, and re-layouts  5.08 us (6%)
  between operations  3.04 us (3%)
    pallas_call x1, Pallas kernels, local(): pl.pallas_call(functools.partial(body, n_mpo, n_sec), out_shape=(jax.Shap...  82.6 us
    unnamed x8, local copies, waits for them, and re-layouts  5.08 us

profile of v1, /device:TPU:0, one launch (start us, length us, event | category | flops | bytes accessed | tf_op | source)
XLA Modules:
  0.0 90.7 jit_solution(12257014269194082965)
XLA Ops:
  1.3 0.0 copy-start
  1.3 1.6 %copy-done = bf16[2,1,512,1024]{3,2,1,0:T(8,128)(2,1)S(1)} copy-done((bf16[2,1,512,1024]{3,2,1,0:T(8,128)(2,1)S(1)}, bf16[2,1,512,1024]{3,2,1,0:T(8,128)(2,1)}, u32[]{:S(2)}) %copy-start) | copy-done | bytes 2097176
  2.9 0.0 copy-start.1
  2.9 1.0 %copy-done.1 = f32[1,512,256]{2,1,0:T(8,128)S(1)} copy-done((f32[1,512,256]{2,1,0:T(8,128)S(1)}, f32[1,512,256]{2,1,0:T(8,128)}, u32[]{:S(2)}) %copy-start.1) | copy-done | bytes 524312
  3.9 0.0 copy-start.2
  3.9 0.9 %copy-done.2 = bf16[2,1,256,256]{3,2,1,0:T(8,128)(2,1)S(1)} copy-done((bf16[2,1,256,256]{3,2,1,0:T(8,128)(2,1)S(1)}, bf16[2,1,256,256]{3,2,1,0:T(8,128)(2,1)}, u32[]{:S(2)}) %copy-start.2) | copy-done | bytes 262168
  4.9 82.6 %shard_map.67 = (f32[1,512,256]{2,1,0:T(8,128)S(1)}, f32[1]{0:T(128)}, f32[2,1,128,256]{3,2,1,0:T(8,128)S(1)}) custom-call(s32[1]{0:T(128)S(6)} %copy.10.block_rows, f32[1,512,256]{2,1,0:T(8,128)S(1)} %copy-done.1, bf16[2,1,512,1024]{3,2,1,0:T(8,128)(2,1)S(1)} %copy-done, bf16[2,1,256,256]{3,2,1,0:T(8,128)(2,1)S(1)} %copy-done.2), custom_call_target="tpu_custom_call" | custom-call | tf_op jit(solution)/shard_map/pallas_call | solution.py:467
  87.4 0.8 copy.11
  88.8 0.7 copy.13
Async XLA Ops:
  1.3 1.6 %copy-start = (bf16[2,1,512,1024]{3,2,1,0:T(8,128)(2,1)S(1)}, bf16[2,1,512,1024]{3,2,1,0:T(8,128)(2,1)}, u32[]{:S(2)}) copy-start(bf16[2,1,512,1024]{3,2,1,0:T(8,128)(2,1)} %left_hbm.1) | copy-start | bytes 6291460
  2.9 1.0 %copy-start.1 = (f32[1,512,256]{2,1,0:T(8,128)S(1)}, f32[1,512,256]{2,1,0:T(8,128)}, u32[]{:S(2)}) copy-start(f32[1,512,256]{2,1,0:T(8,128)} %start_hbm.1) | copy-start | bytes 1572868
  3.9 0.9 %copy-start.2 = (bf16[2,1,256,256]{3,2,1,0:T(8,128)(2,1)S(1)}, bf16[2,1,256,256]{3,2,1,0:T(8,128)(2,1)}, u32[]{:S(2)}) copy-start(bf16[2,1,256,256]{3,2,1,0:T(8,128)(2,1)} %right_hbm.1) | copy-start | bytes 786436

commit v2 on v1

--- a/solution.py
+++ b/solution.py
@@ -11,9 +11,9 @@
 ITERS = 4
 EPSILON = 1e-06
 STEPS = ITERS + 1
-CHUNKS = 8
+CHUNKS = 16
 BLOCKS = 4
-LAG = 2
+LAG = 8
 
 F32 = jnp.float32
 BF16 = jnp.bfloat16
@@ -473,9 +473,9 @@
         ),
         in_specs=[
             pl.BlockSpec(memory_space=pltpu.SMEM),
-            pl.BlockSpec(memory_space=pl.ANY),
-            pl.BlockSpec(memory_space=pl.ANY),
-            pl.BlockSpec(memory_space=pl.ANY),
+            pl.BlockSpec(memory_space=pltpu.HBM),
+            pl.BlockSpec(memory_space=pltpu.HBM),
+            pl.BlockSpec(memory_space=pltpu.HBM),
         ],
         out_specs=(
             pl.BlockSpec(memory_space=pltpu.VMEM),
@@ -516,7 +516,7 @@
             dma,
         ],
         compiler_params=pltpu.CompilerParams(
-            collective_id=0, has_side_effects=True, vmem_limit_bytes=50 * 2**20
+            collective_id=0, has_side_effects=True, vmem_limit_bytes=62 * 2**20
         ),
     )(block_rows, start_vector, left_blocks, right_blocks)
 

time: 90.9 us -> 82 us (0.902)
  Pallas kernels: 82.6 us -> 75.2 us
  local copies, waits for them, and re-layouts: 5.08 us -> 3.54 us
    pallas_call x1, Pallas kernels: 82.6 us -> 75.2 us  [local(): pl.pallas_call(functools.partial(body, n_mpo, n_sec), out_shape=(jax.Shap...]
    unnamed x8 -> x2, local copies, waits for them, and re-layouts: 5.08 us -> 3.54 us
where the time goes in v2:
time: 82 us; the launch traced here: 81.7 us
  Pallas kernels  75.2 us (92%)
  local copies, waits for them, and re-layouts  3.54 us (4%)
  between operations  2.97 us (4%)
    pallas_call x1, Pallas kernels, local(): pl.pallas_call(functools.partial(body, n_mpo, n_sec), out_shape=(jax.Shap...  75.2 us
    unnamed x2, local copies, waits for them, and re-layouts  3.54 us

profile of v2, /device:TPU:0, one launch (start us, length us, event | category | flops | bytes accessed | tf_op | source)
XLA Modules:
  0.0 81.7 jit_solution(6264904967219050726)
XLA Ops:
  1.3 75.2 %shard_map.67 = (f32[1,512,256]{2,1,0:T(8,128)}, f32[1]{0:T(128)}, f32[2,1,128,256]{3,2,1,0:T(8,128)}) custom-call(s32[1]{0:T(128)S(6)} %copy.10.block_rows, f32[1,512,256]{2,1,0:T(8,128)} %start_hbm.1, bf16[2,1,512,1024]{3,2,1,0:T(8,128)(2,1)} %left_hbm.1, bf16[2,1,256,256]{3,2,1,0:T(8,128)(2,1)} %right_hbm.1), custom_call_target="tpu_custom_call" | custom-call | tf_op jit(solution)/shard_map/pallas_call | solution.py:467
  76.5 1.9 %copy.11 = f32[1,512,256]{2,1,0:T(8,128)} copy(f32[1,512,256]{2,1,0:T(8,128)} %get-tuple-element.6) | data formatting | bytes 1048576
  78.9 1.7 %copy.13 = f32[2,1,128,256]{3,2,1,0:T(8,128)} copy(f32[2,1,128,256]{3,2,1,0:T(8,128)} %get-tuple-element.8) | data formatting | bytes 524288

commit v3 on v2

--- a/solution.py
+++ b/solution.py
@@ -13,7 +13,7 @@
 STEPS = ITERS + 1
 CHUNKS = 16
 BLOCKS = 4
-LAG = 8
+LAG = 7
 
 F32 = jnp.float32
 BF16 = jnp.bfloat16
@@ -304,38 +304,7 @@
             result[i] = scaled if i not in result else result[i] + scaled
         return result
 
-    start_load.wait()
-    pl.semaphore_wait(barrier, n_all - 1)
-    acc[...] = jnp.zeros_like(acc)
-
-    def begin(c, carry):
-        at = pl.multiple_of(c * chunk, chunk)
-        put_basis(0, c, jnp.where(live_of(c), start_v[pl.ds(at, chunk)], 0.0))
-        return carry
-
-    lax.fori_loop(0, CHUNKS, begin, 0)
-    share_gram(0)
-    left_load.wait()
-    right_load.wait()
-
-    state = {}
-    for k in range(STEPS):
-        x_copy(k, other_at, rows).wait_recv()
-        if k == ITERS:
-            acc[...] = jnp.zeros_like(acc)
-        multiply(k)
-        if k == ITERS:
-            last[every] = jnp.broadcast_to(whole(acc[0])[:, :128], (8, 128))
-
-            def send_last(d, carry):
-                last_copy(d, True).start()
-                return carry
-
-            lax.fori_loop(1, n_all, send_last, 0)
-        for j, value in enumerate(take_gram(k)):
-            grams[(j, k)] = value
-        if k < ITERS:
-            inverse = coefficients(k)
+    def advance(k, state):
         if k == 0:
             first = lax.rsqrt(g(0, 0) + EPSILON)
             state["vector"] = {0: first}
@@ -365,10 +334,48 @@
                 vector=vector, applied=applied, rayleigh=rayleigh, residual=residual,
                 square_sum=square_sum, scale=scale, coupling=square_sum / scale,
             )
+        return state
+
+    start_load.wait()
+    pl.semaphore_wait(barrier, n_all - 1)
+    acc[...] = jnp.zeros_like(acc)
+
+    def begin(c, carry):
+        at = pl.multiple_of(c * chunk, chunk)
+        put_basis(0, c, jnp.where(live_of(c), start_v[pl.ds(at, chunk)], 0.0))
+        return carry
+
+    lax.fori_loop(0, CHUNKS, begin, 0)
+    share_gram(0)
+    left_load.wait()
+    right_load.wait()
+
+    state = {}
+    for k in range(STEPS):
+        x_copy(k, other_at, rows).wait_recv()
+        if k == ITERS:
+            acc[...] = jnp.zeros_like(acc)
+        multiply(k)
+        if k == ITERS:
+            last[every] = jnp.broadcast_to(whole(acc[0])[:, :128], (8, 128))
+
+            def send_last(d, carry):
+                last_copy(d, True).start()
+                return carry
+
+            lax.fori_loop(1, n_all, send_last, 0)
+        if k >= 1:
+            state = advance(k - 1, state)
+        for j, value in enumerate(take_gram(k)):
+            grams[(j, k)] = value
+        if k < ITERS:
+            inverse = coefficients(k)
         if k < ITERS:
             acc[...] = jnp.zeros_like(acc)
             combine(k, inverse)
             share_gram(k + 1)
+
+    state = advance(ITERS, state)
 
     vector, rayleigh, residual = state["vector"], state["rayleigh"], state["residual"]
     scale, coupling = state["scale"], state["coupling"]

time: 82 us -> 81.6 us (level)
  no operation moved by 1% of the time
where the time goes in v3:
time: 81.6 us; the launch traced here: 81.3 us
  Pallas kernels  74.8 us (92%)
  local copies, waits for them, and re-layouts  3.54 us (4%)
  between operations  2.97 us (4%)
    pallas_call x1, Pallas kernels, local(): pl.pallas_call(functools.partial(body, n_mpo, n_sec), out_shape=(jax.Shap...  74.8 us
    unnamed x2, local copies, waits for them, and re-layouts  3.54 us

profile of v3, /device:TPU:0, one launch (start us, length us, event | category | flops | bytes accessed | tf_op | source)
XLA Modules:
  0.0 81.3 jit_solution(3472337929052363250)
XLA Ops:
  1.3 74.8 %shard_map.67 = (f32[1,512,256]{2,1,0:T(8,128)}, f32[1]{0:T(128)}, f32[2,1,128,256]{3,2,1,0:T(8,128)}) custom-call(s32[1]{0:T(128)S(6)} %copy.10.block_rows, f32[1,512,256]{2,1,0:T(8,128)} %start_hbm.1, bf16[2,1,512,1024]{3,2,1,0:T(8,128)(2,1)} %left_hbm.1, bf16[2,1,256,256]{3,2,1,0:T(8,128)(2,1)} %right_hbm.1), custom_call_target="tpu_custom_call" | custom-call | tf_op jit(solution)/shard_map/pallas_call | solution.py:474
  76.1 1.9 %copy.11 = f32[1,512,256]{2,1,0:T(8,128)} copy(f32[1,512,256]{2,1,0:T(8,128)} %get-tuple-element.6) | data formatting | bytes 1048576
  78.5 1.7 %copy.13 = f32[2,1,128,256]{3,2,1,0:T(8,128)} copy(f32[2,1,128,256]{3,2,1,0:T(8,128)} %get-tuple-element.8) | data formatting | bytes 524288
